TPU v7x, 256 devices: a whole 4x4x8 slice. The times are simulated.
256 devices in a mesh: grp: 4 (over z_lo), seq: 64 (over x, z_hi, y, core).
Axes of the slice: x: 4, y: 4, z: 8 (z_hi: 2, z_lo: 4; z = z_hi * 4 + z_lo), core: 2. Of those that a mesh axis runs over, the one named last changes fastest.
Arguments:
- queries: bfloat16 [65536, 2560], P(('grp', 'seq')), may hold values from -150 to 150, as said below
- key_matrix: bfloat16 [65536, 2560], P(('grp', 'seq')), may hold values from -4 to 4, as said below
- value_matrix: bfloat16 [65536, 2560], P(('grp', 'seq')), may hold values from -6 to 6
Outputs:
- attended: bfloat16 [65536, 2560], P(('grp', 'seq'))
Inputs may be any that keep to these rules, and one draw needn't show every extreme that they name: `key_matrix`: keys are of order one. `queries`: queries are of order one in the shown draw.
All inputs are finite; a program needn't handle non-finite values.
Results may differ from a plain program's by a relative error of at most 0.001.
The roundings to bfloat16 on the way count: a program that leaves them out, or rounds other values in their place, can miss the bound.
Values may be sent and summed in bfloat16 or wider, within the bound.
A program may use at most 128 MiB of HBM per device.

v0:
```python
import functools

import jax
import jax.numpy as jnp
from jax import lax
from jax.experimental import pallas as pl
from jax.experimental.pallas import tpu as pltpu
from jax.sharding import PartitionSpec as P

HEADS = 32
HEAD = 80
WIDTH = HEADS * HEAD
ROWS = 256
COARSE = 16
WHOLE = 128
LANES = 128
GROUP = 8
SPAN = GROUP * HEAD
GROUPS = HEADS // GROUP
SEQ = 64
GRP = 4
PICKS = ROWS // COARSE
COARSE_ROWS = SEQ * PICKS
FAR = ROWS // WHOLE * SEQ
SCALE = HEAD**-0.5
LOG2E = 1.4426950408889634
LOWEST = -1e30
MESH = pl.DeviceIdType.MESH
F32, BF16 = jnp.float32, jnp.bfloat16

NT = (((1,), (1,)), ((), ()))
NN = (((1,), (0,)), ((), ()))


def dot(a, b, dims=NN):
    return lax.dot_general(a, b, dims, preferred_element_type=F32)


def iota(shape, axis):
    return lax.broadcasted_iota(jnp.int32, shape, axis)


def head_of(lane):
    return (lane * 52429) >> 22


def eye(n):
    return jnp.where(iota((n, n), 0) == iota((n, n), 1), 1.0, 0.0).astype(BF16)


def window(hh):
    tile, shift = HEAD * hh // LANES, HEAD * hh % LANES
    return tile, shift, 1 if shift + HEAD <= LANES else 2


def in_circle(lane, start, length):
    return ((lane - start) & (LANES - 1)) < length


def group_mask(group):
    shape = (COARSE, SPAN)
    residue = (head_of(iota(shape, 1)) + group * GROUP) & (COARSE - 1)
    return jnp.where(iota(shape, 0) == residue, 1.0, 0.0).astype(BF16)


def pick(x, mask, gather):
    masked = (x.reshape(PICKS, COARSE, SPAN) * mask[None]).reshape(ROWS, SPAN)
    return dot(gather, masked)


def pack_group(group, q, k, v, mask, gather, send, q_pick):
    lane = iota((PICKS, LANES), 1)
    qp, kp, vp = (pick(x, mask, gather) for x in (q, k, v))
    q_pick[group] = qp.astype(BF16)
    for hh in range(GROUP):
        tile, shift, tiles = window(hh)

        def circle(x):
            first = x[:, LANES * tile : LANES * (tile + 1)]
            if tiles == 1:
                return first
            return jnp.where(lane >= shift, first, x[:, LANES * (tile + 1) : LANES * (tile + 2)])

        own = in_circle(lane, shift, HEAD)
        vc = circle(vp)
        head = group * GROUP + hh
        send[head, :, :LANES] = jnp.where(own, circle(kp), pltpu.roll(vc, HEAD, 1)).astype(BF16)
        send[head, :, LANES:] = jnp.where(own, circle(qp), pltpu.roll(vc, 32, 1)).astype(BF16)


def local_group(group, q, k, v, out):
    unit = eye(LANES)
    half = ROWS // 2
    v_t = jnp.concatenate(
        [dot(unit, v[:, LANES * j : LANES * (j + 1)], NT).astype(BF16) for j in range(SPAN // LANES)], axis=0
    )
    allowed = iota((half, half), 0) <= iota((half, half), 1)
    parts = []
    for hh in range(GROUP):
        tile, shift, tiles = window(hh)
        cols = slice(LANES * tile, LANES * (tile + tiles))
        lane = iota((1, LANES * tiles), 1)
        own = jnp.where((lane >= shift) & (lane < shift + HEAD), 1.0, 0.0).astype(BF16)
        s = dot(k[:, cols], q[:, cols] * own, NT)
        s00 = jnp.where(allowed, s[:half, :half], LOWEST)
        s01 = s[:half, half:]
        s11 = jnp.where(allowed, s[half:, half:], LOWEST)
        top0 = jnp.max(s00, axis=0, keepdims=True)
        top1 = jnp.maximum(jnp.max(s01, axis=0, keepdims=True), jnp.max(s11, axis=0, keepdims=True))
        w00 = jnp.exp2((s00 - top0) * (SCALE * LOG2E))
        w01 = jnp.exp2((s01 - top1) * (SCALE * LOG2E))
        w11 = jnp.exp2((s11 - top1) * (SCALE * LOG2E))
        mass0 = jnp.sum(w00, axis=0, keepdims=True)
        mass1 = jnp.sum(w01, axis=0, keepdims=True) + jnp.sum(w11, axis=0, keepdims=True)
        w = jnp.concatenate(
            [
                jnp.concatenate([w00.astype(BF16), w01.astype(BF16)], axis=1),
                jnp.concatenate([jnp.zeros((half, half), BF16), w11.astype(BF16)], axis=1),
            ],
            axis=0,
        )
        o = dot(v_t[HEAD * hh : HEAD * (hh + 1)], w)
        o = o * (1.0 / jnp.concatenate([mass0, mass1], axis=1))
        parts.append(o.astype(BF16))
    turned = jnp.concatenate(parts, axis=0)
    unit = eye(ROWS)
    for j in range(SPAN // LANES):
        cols = pl.ds(pl.multiple_of(group * SPAN + LANES * j, LANES), LANES)
        out[:, cols] = dot(unit, turned[LANES * j : LANES * (j + 1)], NT).astype(BF16)


def local_picks(group, q_pick, k, v, o_pick, lse_pick):
    shape = (GROUP * PICKS, SPAN)
    own = (iota(shape, 0) >> 4) == head_of(iota(shape, 1))
    q = jnp.concatenate([q_pick] * GROUP, axis=0) * jnp.where(own, 1.0, 0.0).astype(BF16)
    s = dot(q, k, NT)
    row, key = iota(s.shape, 0), iota(s.shape, 1)
    residue = ((row >> 4) + group * GROUP) & (COARSE - 1)
    s = jnp.where(key <= (row & (PICKS - 1)) * COARSE + residue, s, LOWEST)
    top = jnp.max(s, axis=1, keepdims=True)
    w = jnp.exp2((s - top) * (SCALE * LOG2E))
    mass = jnp.sum(w, axis=1, keepdims=True)
    o = dot(w.astype(BF16), v) * (1.0 / mass)
    lse = top * SCALE + jnp.log(mass)
    cols = pl.ds(pl.multiple_of(group * SPAN, LANES), SPAN)
    o_pick[:, cols] = jnp.sum(jnp.where(own, o, 0.0).reshape(GROUP, PICKS, SPAN), axis=0)
    lse_pick[:, cols] = jnp.sum(jnp.where(own, lse, 0.0).reshape(GROUP, PICKS, SPAN), axis=0)


def attend(q, keys, allowed, lane, turn):
    s = dot(q, keys[:, :LANES], NT)
    s = allowed(s)
    top = jnp.max(s, axis=1, keepdims=True)
    w = jnp.exp2((s - top) * (SCALE * LOG2E))
    mass = jnp.sum(w, axis=1, keepdims=True)
    both = dot(w.astype(BF16), keys)
    o = jnp.where(in_circle(lane, turn + HEAD, 48), both[:, :LANES], pltpu.roll(both[:, LANES:], 48, 1))
    o = o * (1.0 / mass)
    lse = top * SCALE + jnp.log(mass)
    return jnp.where(in_circle(lane, turn + HEAD, HEAD), o, lse)


def coarse_blocks(head, recv, back):
    turn = lax.rem(head * HEAD, LANES)
    lane = iota((1, LANES), 1)
    own = jnp.where(in_circle(lane, turn, HEAD), 1.0, 0.0).astype(BF16)
    x = recv[...].reshape(COARSE_ROWS, 2 * LANES)
    step = 256
    below = iota((step, step), 1) <= iota((step, step), 0)
    for b in range(COARSE_ROWS // step):
        def allowed(s):
            last = jnp.where(below, s[:, step * b :], LOWEST)
            return last if b == 0 else jnp.concatenate([s[:, : step * b], last], axis=1)

        q = x[step * b : step * (b + 1), LANES:] * own
        back[step * b : step * (b + 1), :] = attend(q, x[: step * (b + 1)], allowed, iota((step, LANES), 1), turn)


def far_rows(head, grp, recv, far):
    block = 256
    per = block // 8
    chosen = iota((per, block), 1) == iota((per, block), 0) * 8 + head // COARSE
    chosen = jnp.where(chosen, 1.0, 0.0).astype(BF16)
    for b in range(COARSE_ROWS // block):
        x = recv[block // PICKS * b : block // PICKS * (b + 1)].reshape(block, 2 * LANES)
        far[grp, per * b : per * (b + 1), :] = dot(chosen, x).astype(BF16)


def whole_level(head, grp, far, back):
    turn = lax.rem(head * HEAD, LANES)
    lane = iota((1, LANES), 1)
    own = jnp.where(in_circle(lane, turn, HEAD), 1.0, 0.0).astype(BF16)
    keys = far[...].reshape(GRP * FAR, 2 * LANES)
    q = far[grp, :, LANES:] * own

    def allowed(s):
        return jnp.where(iota(s.shape, 1) <= iota(s.shape, 0) + grp * FAR, s, LOWEST)

    lane = iota((FAR, LANES), 1)
    mine = attend(q, keys, allowed, lane, turn)
    rows = pl.ds(head // COARSE, FAR, stride=8)
    other = back[rows, :]
    result = in_circle(lane, turn + HEAD, HEAD)
    l2 = jnp.max(jnp.where(result, LOWEST * 2, other), axis=1, keepdims=True)
    l3 = jnp.max(jnp.where(result, LOWEST * 2, mine), axis=1, keepdims=True)
    best = jnp.maximum(l2, l3)
    e2, e3 = jnp.exp(l2 - best), jnp.exp(l3 - best)
    total = e2 + e3
    back[rows, :] = jnp.where(result, (e2 * other + e3 * mine) / total, best + jnp.log(total))


def merge_group(group, home, o_pick, lse_pick, out):
    lane = iota((PICKS, LANES), 1)
    tiles_o = [jnp.zeros((PICKS, LANES), F32)] * (SPAN // LANES)
    tiles_l = list(tiles_o)
    for hh in range(GROUP):
        tile, shift, tiles = window(hh)
        m = home[group * GROUP + hh]
        o = pltpu.roll(m, 48, 1)
        at = (shift + 40) % LANES
        lse = jnp.broadcast_to(m[:, at : at + 1], (PICKS, LANES))
        for n in range(tiles):
            here = lane >= shift if n == 0 else lane < shift + HEAD - LANES
            tiles_o[tile + n] = jnp.where(here, o, tiles_o[tile + n])
            tiles_l[tile + n] = jnp.where(here, lse, tiles_l[tile + n])
    for n in range(SPAN // LANES):
        cols = pl.ds(pl.multiple_of(group * SPAN + n * LANES, LANES), LANES)
        l1, l2 = lse_pick[:, cols], tiles_l[n]
        best = jnp.maximum(l1, l2)
        e1, e2 = jnp.exp(l1 - best), jnp.exp(l2 - best)
        merged = (e1 * o_pick[:, cols] + e2 * tiles_o[n]) / (e1 + e2)
        shape = (PICKS, COARSE, LANES)
        residue = head_of(iota((1, COARSE, LANES), 2) + (group * SPAN + n * LANES)) & (COARSE - 1)
        chosen = iota((1, COARSE, LANES), 1) == residue
        rows = jnp.where(chosen, merged.reshape(PICKS, 1, LANES), out[:, cols].reshape(shape).astype(F32))
        out[:, cols] = rows.reshape(ROWS, LANES).astype(BF16)


def kernel(
    q_hbm, k_hbm, v_hbm, out,
    q, k, v, q_pick, o_pick, lse_pick, send, recv, far, back, home,
    in_sem, send_sem, recv_sem, far_send, far_recv, back_send, home_recv,
):
    grp, seq = lax.axis_index("grp"), lax.axis_index("seq")
    head = seq // 2
    owner = lax.rem(seq, 2) == 0

    def loads(group):
        cols = pl.ds(pl.multiple_of(group * SPAN, LANES), SPAN)
        return [
            pltpu.make_async_copy(x.at[:, cols], y.at[:, cols], in_sem.at[group, n])
            for n, (x, y) in enumerate(((q_hbm, q), (k_hbm, k), (v_hbm, v)))
        ]

    for group in range(GROUPS):
        for copy in loads(group):
            copy.start()

    barrier = pltpu.get_barrier_semaphore()

    def greet(s, _):
        @pl.when((s != seq) & (owner | (lax.rem(s, 2) == 0)))
        def _():
            pl.semaphore_signal(barrier, inc=1, device_id=(grp, s), device_id_type=MESH)
        return 0

    lax.fori_loop(0, SEQ, greet, 0)

    @pl.when(owner)
    def _():
        for d in range(1, GRP):
            pl.semaphore_signal(barrier, inc=1, device_id=(lax.rem(grp + d, GRP), seq), device_id_type=MESH)

    gather = jnp.where((iota((PICKS, ROWS), 1) >> 4) == iota((PICKS, ROWS), 0), 1.0, 0.0).astype(BF16)

    def pack(group, _):
        for copy in loads(group):
            copy.wait()
        cols = pl.ds(pl.multiple_of(group * SPAN, LANES), SPAN)
        pack_group(group, q[:, cols], k[:, cols], v[:, cols], group_mask(group), gather, send, q_pick)
        return 0

    lax.fori_loop(0, GROUPS, pack, 0)

    @pl.when(owner)
    def _():
        pl.semaphore_wait(barrier, SEQ - 1 + GRP - 1)

    @pl.when(jnp.logical_not(owner))
    def _():
        pl.semaphore_wait(barrier, HEADS)

    def share(j, _):
        h = lax.rem(head + 1 + j, HEADS)

        @pl.when(2 * h != seq)
        def _():
            pltpu.make_async_remote_copy(
                src_ref=send.at[h], dst_ref=recv.at[seq], send_sem=send_sem, recv_sem=recv_sem,
                device_id=(grp, 2 * h), device_id_type=MESH,
            ).start()

        @pl.when(2 * h == seq)
        def _():
            pltpu.make_async_copy(send.at[h], recv.at[seq], recv_sem).start()
        return 0

    lax.fori_loop(0, HEADS, share, 0)

    def local(group, _):
        cols = pl.ds(pl.multiple_of(group * SPAN, LANES), SPAN)
        local_picks(group, q_pick[group], k[:, cols], v[:, cols], o_pick, lse_pick)
        local_group(group, q[:, cols], k[:, cols], v[:, cols], out)
        return 0

    lax.fori_loop(0, GROUPS, local, 0)

    @pl.when(owner)
    def _():
        pltpu.make_async_copy(recv, recv, recv_sem).wait()
        far_rows(head, grp, recv, far)
        for g in range(1, GRP):
            @pl.when(grp < g)
            def _():
                far[g] = jnp.zeros((FAR, 2 * LANES), BF16)

        def far_copy(to):
            return pltpu.make_async_remote_copy(
                src_ref=far.at[grp], dst_ref=far.at[grp], send_sem=far_send.at[to], recv_sem=far_recv.at[grp],
                device_id=(to, seq), device_id_type=MESH,
            )

        for to in range(1, GRP):
            @pl.when(to > grp)
            def _():
                far_copy(to).start()

        coarse_blocks(head, recv, back)
        for g in range(GRP - 1):
            @pl.when(grp > g)
            def _():
                pltpu.make_async_copy(far.at[g], far.at[g], far_recv.at[g]).wait()
        whole_level(head, grp, far, back)

        def home_copy(j, _):
            s = lax.rem(seq + 1 + j, SEQ)
            rows = pl.ds(pl.multiple_of(s * PICKS, PICKS), PICKS)
            pltpu.make_async_remote_copy(
                src_ref=back.at[rows], dst_ref=home.at[head], send_sem=back_send, recv_sem=home_recv,
                device_id=(grp, s), device_id_type=MESH,
            ).start()
            return 0

        lax.fori_loop(0, SEQ - 1, home_copy, 0)
        rows = pl.ds(pl.multiple_of(seq * PICKS, PICKS), PICKS)
        pltpu.make_async_copy(back.at[rows], home.at[head], home_recv).start()

    pltpu.make_async_copy(home, home, home_recv).wait()

    def merge(group, _):
        merge_group(group, home, o_pick, lse_pick, out)
        return 0

    lax.fori_loop(0, GROUPS, merge, 0)

    @pl.when(owner)
    def _():
        most = send.at[pl.ds(0, HEADS - 1)]
        pltpu.make_async_copy(most, most, send_sem).wait()
        for to in range(1, GRP):
            @pl.when(to > grp)
            def _():
                pltpu.make_async_copy(far.at[0], far.at[0], far_send.at[to]).wait()
        most = back.at[pl.ds(0, (SEQ - 1) * PICKS)]
        pltpu.make_async_copy(most, most, back_send).wait()

    @pl.when(jnp.logical_not(owner))
    def _():
        pltpu.make_async_copy(send, send, send_sem).wait()


def body(queries, key_matrix, value_matrix):
    return pl.pallas_call(
        kernel,
        out_shape=jax.ShapeDtypeStruct((ROWS, WIDTH), BF16),
        in_specs=[pl.BlockSpec(memory_space=pltpu.HBM)] * 3,
        out_specs=pl.BlockSpec(memory_space=pltpu.VMEM),
        scratch_shapes=[
            pltpu.VMEM((ROWS, WIDTH), BF16),
            pltpu.VMEM((ROWS, WIDTH), BF16),
            pltpu.VMEM((ROWS, WIDTH), BF16),
            pltpu.VMEM((GROUPS, PICKS, SPAN), BF16),
            pltpu.VMEM((PICKS, WIDTH), F32),
            pltpu.VMEM((PICKS, WIDTH), F32),
            pltpu.VMEM((HEADS, PICKS, 2 * LANES), BF16),
            pltpu.VMEM((SEQ, PICKS, 2 * LANES), BF16),
            pltpu.VMEM((GRP, FAR, 2 * LANES), BF16),
            pltpu.VMEM((COARSE_ROWS, LANES), F32),
            pltpu.VMEM((HEADS, PICKS, LANES), F32),
            pltpu.SemaphoreType.DMA((GROUPS, 3)),
            pltpu.SemaphoreType.DMA,
            pltpu.SemaphoreType.DMA,
            pltpu.SemaphoreType.DMA((GRP,)),
            pltpu.SemaphoreType.DMA((GRP,)),
            pltpu.SemaphoreType.DMA,
            pltpu.SemaphoreType.DMA,
        ],
        compiler_params=pltpu.CompilerParams(
            collective_id=0, has_side_effects=True, vmem_limit_bytes=48 * 1024 * 1024
        ),
    )(*(pltpu.with_memory_space_constraint(x, pltpu.HBM) for x in (queries, key_matrix, value_matrix)))


def solution(mesh):
    placed = P(("grp", "seq"), None)
    return jax.shard_map(
        body, mesh=mesh, in_specs=(placed,) * 3, out_specs=placed, check_vma=False
    )
```

profile of v0, /device:TPU:64, one launch (start us, length us, event | category | flops | bytes accessed | tf_op | source)
XLA Modules:
  0.0 39.5 jit_solution(2314310141672424412)
XLA Ops:
  0.0 38.5 %shard_map.37 = bf16[256,2560]{1,0:T(8,128)(2,1)S(1)} custom-call(bf16[256,2560]{1,0:T(8,128)(2,1)} %q_hbm.1, bf16[256,2560]{1,0:T(8,128)(2,1)} %k_hbm.1, bf16[256,2560]{1,0:T(8,128)(2,1)} %v_hbm.1), custom_call_target="tpu_custom_call" | custom-call | tf_op jit(solution)/shard_map/pallas_call | solution.py:383
  38.5 1.1 %copy.5 = bf16[256,2560]{1,0:T(8,128)(2,1)} copy(bf16[256,2560]{1,0:T(8,128)(2,1)S(1)} %shard_map.37) | data formatting | bytes 2621440
where the time goes:
time: 39.9 us; the launch traced here: 39.5 us
  Pallas kernels  38.5 us (96%)
  local copies, waits for them, and re-layouts  1.06 us (3%)
    pallas_call x1, Pallas kernels, body(): pl.pallas_call(kernel, out_shape=jax.ShapeDtypeStruct((ROWS, WIDTH), BF16...  38.5 us
    unnamed x1, local copies, waits for them, and re-layouts  1.06 us

commit v1 on v0

--- a/solution.py
+++ b/solution.py
@@ -21,7 +21,8 @@
 GRP = 4
 PICKS = ROWS // COARSE
 COARSE_ROWS = SEQ * PICKS
-FAR = ROWS // WHOLE * SEQ
+HALF_ROWS = COARSE_ROWS // 2
+FAR = ROWS // WHOLE * SEQ // 2
 SCALE = HEAD**-0.5
 LOG2E = 1.4426950408889634
 LOWEST = -1e30
@@ -147,57 +148,71 @@
     lse_pick[:, cols] = jnp.sum(jnp.where(own, lse, 0.0).reshape(GROUP, PICKS, SPAN), axis=0)
 
 
-def attend(q, keys, allowed, lane, turn):
-    s = dot(q, keys[:, :LANES], NT)
-    s = allowed(s)
-    top = jnp.max(s, axis=1, keepdims=True)
-    w = jnp.exp2((s - top) * (SCALE * LOG2E))
-    mass = jnp.sum(w, axis=1, keepdims=True)
-    both = dot(w.astype(BF16), keys)
+def attend(q, parts, lane, turn):
+    scores = [hide(dot(q, keys[:, :LANES], NT)) for keys, hide in parts]
+    top = functools.reduce(jnp.maximum, [jnp.max(s, axis=1, keepdims=True) for s in scores])
+    weights = [jnp.exp2((s - top) * (SCALE * LOG2E)) for s in scores]
+    mass = sum(jnp.sum(w, axis=1, keepdims=True) for w in weights)
+    both = sum(dot(w.astype(BF16), keys) for w, (keys, _) in zip(weights, parts))
     o = jnp.where(in_circle(lane, turn + HEAD, 48), both[:, :LANES], pltpu.roll(both[:, LANES:], 48, 1))
     o = o * (1.0 / mass)
     lse = top * SCALE + jnp.log(mass)
     return jnp.where(in_circle(lane, turn + HEAD, HEAD), o, lse)
 
 
-def coarse_blocks(head, recv, back):
+def place(p, half):
+    return (p >> 3) * 16 + half * 8 + (p & 7)
+
+
+def coarse_blocks(head, half, near, other, back):
     turn = lax.rem(head * HEAD, LANES)
-    lane = iota((1, LANES), 1)
-    own = jnp.where(in_circle(lane, turn, HEAD), 1.0, 0.0).astype(BF16)
-    x = recv[...].reshape(COARSE_ROWS, 2 * LANES)
-    step = 256
+    own = jnp.where(in_circle(iota((1, LANES), 1), turn, HEAD), 1.0, 0.0).astype(BF16)
+    step = 128
     below = iota((step, step), 1) <= iota((step, step), 0)
-    for b in range(COARSE_ROWS // step):
-        def allowed(s):
-            last = jnp.where(below, s[:, step * b :], LOWEST)
-            return last if b == 0 else jnp.concatenate([s[:, : step * b], last], axis=1)
-
-        q = x[step * b : step * (b + 1), LANES:] * own
-        back[step * b : step * (b + 1), :] = attend(q, x[: step * (b + 1)], allowed, iota((step, LANES), 1), turn)
-
-
-def far_rows(head, grp, recv, far):
+    x = near[...].reshape(HALF_ROWS, 2 * LANES)
+    y = other[...].reshape(HALF_ROWS, 2 * LANES)
+    for b in range(HALF_ROWS // step):
+        start = b * step
+
+        def last_hidden(s):
+            last = jnp.where(below, s[:, start:], LOWEST)
+            return last if b == 0 else jnp.concatenate([s[:, :start], last], axis=1)
+
+        parts = [(x[: start + step], last_hidden)]
+        if b + half > 0:
+            parts.append((y[: start + half * step], lambda s: s))
+        q = x[start : start + step, LANES:] * own
+        back[start : start + step, :] = attend(q, parts, iota((step, LANES), 1), turn)
+
+
+def far_rows(head, half, grp, recv, far):
     block = 256
     per = block // 8
     chosen = iota((per, block), 1) == iota((per, block), 0) * 8 + head // COARSE
     chosen = jnp.where(chosen, 1.0, 0.0).astype(BF16)
-    for b in range(COARSE_ROWS // block):
+    for b in range(HALF_ROWS // block):
         x = recv[block // PICKS * b : block // PICKS * (b + 1)].reshape(block, 2 * LANES)
-        far[grp, per * b : per * (b + 1), :] = dot(chosen, x).astype(BF16)
-
-
-def whole_level(head, grp, far, back):
+        far[grp, half, per * b : per * (b + 1), :] = dot(chosen, x).astype(BF16)
+
+
+def far_place(r):
+    return (r >> 4) * 32 + (r & 15)
+
+
+def whole_level(head, half, grp, far, back):
     turn = lax.rem(head * HEAD, LANES)
-    lane = iota((1, LANES), 1)
-    own = jnp.where(in_circle(lane, turn, HEAD), 1.0, 0.0).astype(BF16)
-    keys = far[...].reshape(GRP * FAR, 2 * LANES)
-    q = far[grp, :, LANES:] * own
-
-    def allowed(s):
-        return jnp.where(iota(s.shape, 1) <= iota(s.shape, 0) + grp * FAR, s, LOWEST)
+    own = jnp.where(in_circle(iota((1, LANES), 1), turn, HEAD), 1.0, 0.0).astype(BF16)
+    keys = far[...].reshape(GRP * 2 * FAR, 2 * LANES)
+    q = far[grp, half, :, LANES:] * own
+
+    def hide(s):
+        row, col = iota(s.shape, 0), iota(s.shape, 1)
+        row = grp * (2 * FAR) + half * 16 + far_place(row)
+        col = (col >> 7) * (2 * FAR) + ((col >> 6) & 1) * 16 + far_place(col & (FAR - 1))
+        return jnp.where(col <= row, s, LOWEST)
 
     lane = iota((FAR, LANES), 1)
-    mine = attend(q, keys, allowed, lane, turn)
+    mine = attend(q, [(keys, hide)], lane, turn)
     rows = pl.ds(head // COARSE, FAR, stride=8)
     other = back[rows, :]
     result = in_circle(lane, turn + HEAD, HEAD)
@@ -238,12 +253,33 @@
 
 def kernel(
     q_hbm, k_hbm, v_hbm, out,
-    q, k, v, q_pick, o_pick, lse_pick, send, recv, far, back, home,
+    q, k, v, q_pick, o_pick, lse_pick, send, near, other, far, back, home,
     in_sem, send_sem, recv_sem, far_send, far_recv, back_send, home_recv,
 ):
     grp, seq = lax.axis_index("grp"), lax.axis_index("seq")
-    head = seq // 2
-    owner = lax.rem(seq, 2) == 0
+    half = (seq >> 3) & 1
+    head = (seq >> 4) * 8 + (seq & 7)
+    late = (half == 1) & (head >= HEADS - 8)
+
+    barrier = pltpu.get_barrier_semaphore()
+
+    def greet(j, _):
+        p = (head + j) & (HEADS - 1)
+        pl.semaphore_signal(barrier, inc=1, device_id=(grp, place(p, 1 - half)), device_id_type=MESH)
+        return 0
+
+    def greet_near(j, _):
+        p = (head + j) & (HEADS - 1)
+        pl.semaphore_signal(barrier, inc=1, device_id=(grp, place(p, half)), device_id_type=MESH)
+        return 0
+
+    lax.fori_loop(0, HEADS, greet, 0)
+    for d in range(1, GRP):
+        for h in (1 - half, half):
+            pl.semaphore_signal(
+                barrier, inc=1, device_id=(lax.rem(grp + d, GRP), place(head, h)), device_id_type=MESH
+            )
+    lax.fori_loop(1, HEADS, greet_near, 0)
 
     def loads(group):
         cols = pl.ds(pl.multiple_of(group * SPAN, LANES), SPAN)
@@ -256,21 +292,6 @@
         for copy in loads(group):
             copy.start()
 
-    barrier = pltpu.get_barrier_semaphore()
-
-    def greet(s, _):
-        @pl.when((s != seq) & (owner | (lax.rem(s, 2) == 0)))
-        def _():
-            pl.semaphore_signal(barrier, inc=1, device_id=(grp, s), device_id_type=MESH)
-        return 0
-
-    lax.fori_loop(0, SEQ, greet, 0)
-
-    @pl.when(owner)
-    def _():
-        for d in range(1, GRP):
-            pl.semaphore_signal(barrier, inc=1, device_id=(lax.rem(grp + d, GRP), seq), device_id_type=MESH)
-
     gather = jnp.where((iota((PICKS, ROWS), 1) >> 4) == iota((PICKS, ROWS), 0), 1.0, 0.0).astype(BF16)
 
     def pack(group, _):
@@ -282,30 +303,30 @@
 
     lax.fori_loop(0, GROUPS, pack, 0)
 
-    @pl.when(owner)
+    pl.semaphore_wait(barrier, SEQ - 1 + 2 * (GRP - 1))
+
+    def across(j, _):
+        h = (head + j) & (HEADS - 1)
+        pltpu.make_async_remote_copy(
+            src_ref=send.at[h], dst_ref=other.at[head], send_sem=send_sem, recv_sem=recv_sem.at[1],
+            device_id=(grp, place(h, 1 - half)), device_id_type=MESH,
+        ).start()
+        return 0
+
+    def beside(j, _):
+        h = (head + j) & (HEADS - 1)
+        pltpu.make_async_remote_copy(
+            src_ref=send.at[h], dst_ref=near.at[head], send_sem=send_sem, recv_sem=recv_sem.at[0],
+            device_id=(grp, place(h, half)), device_id_type=MESH,
+        ).start()
+        return 0
+
+    @pl.when(jnp.logical_not(late))
     def _():
-        pl.semaphore_wait(barrier, SEQ - 1 + GRP - 1)
-
-    @pl.when(jnp.logical_not(owner))
-    def _():
-        pl.semaphore_wait(barrier, HEADS)
-
-    def share(j, _):
-        h = lax.rem(head + 1 + j, HEADS)
-
-        @pl.when(2 * h != seq)
-        def _():
-            pltpu.make_async_remote_copy(
-                src_ref=send.at[h], dst_ref=recv.at[seq], send_sem=send_sem, recv_sem=recv_sem,
-                device_id=(grp, 2 * h), device_id_type=MESH,
-            ).start()
-
-        @pl.when(2 * h == seq)
-        def _():
-            pltpu.make_async_copy(send.at[h], recv.at[seq], recv_sem).start()
-        return 0
-
-    lax.fori_loop(0, HEADS, share, 0)
+        lax.fori_loop(0, HEADS, across, 0)
+
+    lax.fori_loop(1, HEADS, beside, 0)
+    pltpu.make_async_copy(send.at[head], near.at[head], recv_sem.at[0]).start()
 
     def local(group, _):
         cols = pl.ds(pl.multiple_of(group * SPAN, LANES), SPAN)
@@ -313,70 +334,91 @@
         local_group(group, q[:, cols], k[:, cols], v[:, cols], out)
         return 0
 
-    lax.fori_loop(0, GROUPS, local, 0)
-
-    @pl.when(owner)
+    lax.fori_loop(0, GROUPS // 2, local, 0)
+
+    for g in range(1, GRP):
+        @pl.when(grp < g)
+        def _():
+            far[g] = jnp.zeros((2, FAR, 2 * LANES), BF16)
+
+    @pl.when(half == 0)
     def _():
-        pltpu.make_async_copy(recv, recv, recv_sem).wait()
-        far_rows(head, grp, recv, far)
-        for g in range(1, GRP):
-            @pl.when(grp < g)
-            def _():
-                far[g] = jnp.zeros((FAR, 2 * LANES), BF16)
-
-        def far_copy(to):
-            return pltpu.make_async_remote_copy(
-                src_ref=far.at[grp], dst_ref=far.at[grp], send_sem=far_send.at[to], recv_sem=far_recv.at[grp],
-                device_id=(to, seq), device_id_type=MESH,
-            )
-
-        for to in range(1, GRP):
-            @pl.when(to > grp)
-            def _():
-                far_copy(to).start()
-
-        coarse_blocks(head, recv, back)
-        for g in range(GRP - 1):
-            @pl.when(grp > g)
-            def _():
-                pltpu.make_async_copy(far.at[g], far.at[g], far_recv.at[g]).wait()
-        whole_level(head, grp, far, back)
-
-        def home_copy(j, _):
-            s = lax.rem(seq + 1 + j, SEQ)
-            rows = pl.ds(pl.multiple_of(s * PICKS, PICKS), PICKS)
-            pltpu.make_async_remote_copy(
-                src_ref=back.at[rows], dst_ref=home.at[head], send_sem=back_send, recv_sem=home_recv,
-                device_id=(grp, s), device_id_type=MESH,
-            ).start()
-            return 0
-
-        lax.fori_loop(0, SEQ - 1, home_copy, 0)
-        rows = pl.ds(pl.multiple_of(seq * PICKS, PICKS), PICKS)
-        pltpu.make_async_copy(back.at[rows], home.at[head], home_recv).start()
-
-    pltpu.make_async_copy(home, home, home_recv).wait()
+        other[HEADS - 8 :] = jnp.zeros((8, PICKS, 2 * LANES), BF16)
+
+    pltpu.make_async_copy(near, near, recv_sem.at[0]).wait()
+    far_rows(head, half, grp, near, far)
+
+    def far_copy(to, h):
+        return pltpu.make_async_remote_copy(
+            src_ref=far.at[grp, half], dst_ref=far.at[grp, half],
+            send_sem=far_send.at[to, h], recv_sem=far_recv.at[grp, half],
+            device_id=(to, place(head, h)), device_id_type=MESH,
+        )
+
+    for to in range(1, GRP):
+        @pl.when(to > grp)
+        def _():
+            far_copy(to, 1 - half).start()
+            far_copy(to, half).start()
+
+    lax.fori_loop(GROUPS // 2, GROUPS, local, 0)
+
+    @pl.when(half == 0)
+    def _():
+        part = other.at[pl.ds(0, HEADS - 8)]
+        pltpu.make_async_copy(part, part, recv_sem.at[1]).wait()
+        far_rows(head, 1, grp, other, far)
+        coarse_blocks(head, 0, near, other, back)
+
+    @pl.when(half == 1)
+    def _():
+        pltpu.make_async_copy(other, other, recv_sem.at[1]).wait()
+        far_rows(head, 0, grp, other, far)
+        coarse_blocks(head, 1, near, other, back)
+
+    for g in range(GRP - 1):
+        @pl.when(grp > g)
+        def _():
+            for h in range(2):
+                pltpu.make_async_copy(far.at[g, h], far.at[g, h], far_recv.at[g, h]).wait()
+
+    whole_level(head, half, grp, far, back)
+
+    def home_copy(j, _):
+        p = (head + j) & (HEADS - 1)
+        rows = pl.ds(pl.multiple_of(p * PICKS, PICKS), PICKS)
+        pltpu.make_async_remote_copy(
+            src_ref=back.at[rows], dst_ref=home.at[head], send_sem=back_send, recv_sem=home_recv.at[head // GROUP],
+            device_id=(grp, place(p, half)), device_id_type=MESH,
+        ).start()
+        return 0
+
+    lax.fori_loop(1, HEADS, home_copy, 0)
+    rows = pl.ds(pl.multiple_of(head * PICKS, PICKS), PICKS)
+    pltpu.make_async_copy(back.at[rows], home.at[head], home_recv.at[head // GROUP]).start()
 
     def merge(group, _):
+        part = home.at[pl.ds(group * GROUP, GROUP)]
+        pltpu.make_async_copy(part, part, home_recv.at[group]).wait()
         merge_group(group, home, o_pick, lse_pick, out)
         return 0
 
     lax.fori_loop(0, GROUPS, merge, 0)
 
-    @pl.when(owner)
-    def _():
-        most = send.at[pl.ds(0, HEADS - 1)]
-        pltpu.make_async_copy(most, most, send_sem).wait()
-        for to in range(1, GRP):
-            @pl.when(to > grp)
-            def _():
-                pltpu.make_async_copy(far.at[0], far.at[0], far_send.at[to]).wait()
-        most = back.at[pl.ds(0, (SEQ - 1) * PICKS)]
-        pltpu.make_async_copy(most, most, back_send).wait()
-
-    @pl.when(jnp.logical_not(owner))
+    most = send.at[pl.ds(0, HEADS - 1)]
+    pltpu.make_async_copy(most, most, send_sem).wait()
+
+    @pl.when(jnp.logical_not(late))
     def _():
         pltpu.make_async_copy(send, send, send_sem).wait()
+
+    for to in range(1, GRP):
+        @pl.when(to > grp)
+        def _():
+            for h in range(2):
+                pltpu.make_async_copy(far.at[0, 0], far.at[0, 0], far_send.at[to, h]).wait()
+    most = back.at[pl.ds(0, (HEADS - 1) * PICKS)]
+    pltpu.make_async_copy(most, most, back_send).wait()
 
 
 def body(queries, key_matrix, value_matrix):
@@ -393,17 +435,18 @@
             pltpu.VMEM((PICKS, WIDTH), F32),
             pltpu.VMEM((PICKS, WIDTH), F32),
             pltpu.VMEM((HEADS, PICKS, 2 * LANES), BF16),
-            pltpu.VMEM((SEQ, PICKS, 2 * LANES), BF16),
-            pltpu.VMEM((GRP, FAR, 2 * LANES), BF16),
-            pltpu.VMEM((COARSE_ROWS, LANES), F32),
+            pltpu.VMEM((HEADS, PICKS, 2 * LANES), BF16),
+            pltpu.VMEM((HEADS, PICKS, 2 * LANES), BF16),
+            pltpu.VMEM((GRP, 2, FAR, 2 * LANES), BF16),
+            pltpu.VMEM((HALF_ROWS, LANES), F32),
             pltpu.VMEM((HEADS, PICKS, LANES), F32),
             pltpu.SemaphoreType.DMA((GROUPS, 3)),
             pltpu.SemaphoreType.DMA,
+            pltpu.SemaphoreType.DMA((2,)),
+            pltpu.SemaphoreType.DMA((GRP, 2)),
+            pltpu.SemaphoreType.DMA((GRP, 2)),
             pltpu.SemaphoreType.DMA,
-            pltpu.SemaphoreType.DMA((GRP,)),
-            pltpu.SemaphoreType.DMA((GRP,)),
-            pltpu.SemaphoreType.DMA,
-            pltpu.SemaphoreType.DMA,
+            pltpu.SemaphoreType.DMA((GROUPS,)),
         ],
         compiler_params=pltpu.CompilerParams(
             collective_id=0, has_side_effects=True, vmem_limit_bytes=48 * 1024 * 1024

time: 39.9 us -> 37.3 us (0.935)
  the two profiles are of different devices: /device:TPU:64 before, /device:TPU:1 now
where the time goes in v1:
time: 37.3 us
  Pallas kernels  36.2 us (97%)
  local copies, waits for them, and re-layouts  1.06 us (3%)
    pallas_call x1, Pallas kernels, body(): pl.pallas_call(kernel, out_shape=jax.ShapeDtypeStruct((ROWS, WIDTH), BF16...  36.2 us
    unnamed x1, local copies, waits for them, and re-layouts  1.06 us

profile of v1, /device:TPU:1, one launch (start us, length us, event | category | flops | bytes accessed | tf_op | source)
XLA Modules:
  0.0 37.3 jit_solution(2653388057203173233)
XLA Ops:
  0.0 36.2 %shard_map.37 = bf16[256,2560]{1,0:T(8,128)(2,1)S(1)} custom-call(bf16[256,2560]{1,0:T(8,128)(2,1)} %q_hbm.1, bf16[256,2560]{1,0:T(8,128)(2,1)} %k_hbm.1, bf16[256,2560]{1,0:T(8,128)(2,1)} %v_hbm.1), custom_call_target="tpu_custom_call" | custom-call | tf_op jit(solution)/shard_map/pallas_call | solution.py:425
  36.2 1.1 %copy.5 = bf16[256,2560]{1,0:T(8,128)(2,1)} copy(bf16[256,2560]{1,0:T(8,128)(2,1)S(1)} %shard_map.37) | data formatting | bytes 2621440

commit v2 on v1

--- a/solution.py
+++ b/solution.py
@@ -45,6 +45,18 @@
     return (lane * 52429) >> 22
 
 
+def hops(offset):
+    return min(offset, 4 - offset)
+
+
+PLANE = sorted(((dx, dy) for dx in range(4) for dy in range(4)), key=lambda d: -hops(d[0]) - hops(d[1]))
+
+
+def beyond(p, offset):
+    dx, dy = offset
+    return (((p >> 3) + dx) & 3) * 8 + ((p + 2 * dy) & 6) + (p & 1)
+
+
 def eye(n):
     return jnp.where(iota((n, n), 0) == iota((n, n), 1), 1.0, 0.0).astype(BF16)
 
@@ -69,7 +81,7 @@
     return dot(gather, masked)
 
 
-def pack_group(group, q, k, v, mask, gather, send, q_pick):
+def pack_group(group, q, k, v, mask, gather, send, send_pair, q_pick):
     lane = iota((PICKS, LANES), 1)
     qp, kp, vp = (pick(x, mask, gather) for x in (q, k, v))
     q_pick[group] = qp.astype(BF16)
@@ -84,9 +96,17 @@
 
         own = in_circle(lane, shift, HEAD)
         vc = circle(vp)
-        head = group * GROUP + hh
-        send[head, :, :LANES] = jnp.where(own, circle(kp), pltpu.roll(vc, HEAD, 1)).astype(BF16)
-        send[head, :, LANES:] = jnp.where(own, circle(qp), pltpu.roll(vc, 32, 1)).astype(BF16)
+        head, pair = group * GROUP + hh, group * (GROUP // 2) + hh // 2
+        first = jnp.where(own, circle(kp), pltpu.roll(vc, HEAD, 1)).astype(BF16)
+        rest = pltpu.roll(vc, 32, 1)
+        send[head, :, :LANES] = first
+        send[head, :, LANES:] = jnp.where(own, circle(qp), rest).astype(BF16)
+        if hh % 2 == 0:
+            send_pair[pair, :, :LANES] = first
+            even = jnp.where(in_circle(lane, shift + HEAD, 32), rest, 0.0)
+        else:
+            send_pair[pair, :, 2 * LANES :] = first
+            send_pair[pair, :, LANES : 2 * LANES] = jnp.where(in_circle(lane, shift + HEAD, 32), rest, even).astype(BF16)
 
 
 def local_group(group, q, k, v, out):
@@ -164,13 +184,18 @@
     return (p >> 3) * 16 + half * 8 + (p & 7)
 
 
-def coarse_blocks(head, half, near, other, back):
+def other_keys(core, other):
+    first = other[:, :, :, :, pl.ds(pl.multiple_of(core * 2 * LANES, LANES), LANES)]
+    rest = other[:, :, :, :, LANES : 2 * LANES]
+    return jnp.concatenate([x.reshape(HALF_ROWS, LANES) for x in (first, rest)], axis=1)
+
+
+def coarse_blocks(head, half, near, y, back):
     turn = lax.rem(head * HEAD, LANES)
     own = jnp.where(in_circle(iota((1, LANES), 1), turn, HEAD), 1.0, 0.0).astype(BF16)
     step = 128
     below = iota((step, step), 1) <= iota((step, step), 0)
     x = near[...].reshape(HALF_ROWS, 2 * LANES)
-    y = other[...].reshape(HALF_ROWS, 2 * LANES)
     for b in range(HALF_ROWS // step):
         start = b * step
 
@@ -185,14 +210,13 @@
         back[start : start + step, :] = attend(q, parts, iota((step, LANES), 1), turn)
 
 
-def far_rows(head, half, grp, recv, far):
+def far_rows(head, half, grp, x, far):
     block = 256
     per = block // 8
     chosen = iota((per, block), 1) == iota((per, block), 0) * 8 + head // COARSE
     chosen = jnp.where(chosen, 1.0, 0.0).astype(BF16)
     for b in range(HALF_ROWS // block):
-        x = recv[block // PICKS * b : block // PICKS * (b + 1)].reshape(block, 2 * LANES)
-        far[grp, half, per * b : per * (b + 1), :] = dot(chosen, x).astype(BF16)
+        far[grp, half, per * b : per * (b + 1), :] = dot(chosen, x[block * b : block * (b + 1)]).astype(BF16)
 
 
 def far_place(r):
@@ -253,33 +277,25 @@
 
 def kernel(
     q_hbm, k_hbm, v_hbm, out,
-    q, k, v, q_pick, o_pick, lse_pick, send, near, other, far, back, home,
-    in_sem, send_sem, recv_sem, far_send, far_recv, back_send, home_recv,
+    q, k, v, q_pick, o_pick, lse_pick, send, send_pair, near, other, far, back, home,
+    in_sem, send_sem, pair_sem, near_sem, other_sem, pass_send, pass_recv, far_send, far_recv, back_send, home_recv,
 ):
     grp, seq = lax.axis_index("grp"), lax.axis_index("seq")
     half = (seq >> 3) & 1
     head = (seq >> 4) * 8 + (seq & 7)
+    core = head & 1
     late = (half == 1) & (head >= HEADS - 8)
 
     barrier = pltpu.get_barrier_semaphore()
 
-    def greet(j, _):
-        p = (head + j) & (HEADS - 1)
-        pl.semaphore_signal(barrier, inc=1, device_id=(grp, place(p, 1 - half)), device_id_type=MESH)
-        return 0
-
-    def greet_near(j, _):
-        p = (head + j) & (HEADS - 1)
-        pl.semaphore_signal(barrier, inc=1, device_id=(grp, place(p, half)), device_id_type=MESH)
-        return 0
-
-    lax.fori_loop(0, HEADS, greet, 0)
-    for d in range(1, GRP):
-        for h in (1 - half, half):
-            pl.semaphore_signal(
-                barrier, inc=1, device_id=(lax.rem(grp + d, GRP), place(head, h)), device_id_type=MESH
-            )
-    lax.fori_loop(1, HEADS, greet_near, 0)
+    for h in (1, 0):
+        for offset in PLANE:
+            for other_core in (1, 0):
+                if h or other_core or offset != (0, 0):
+                    to = place(beyond(head, offset) ^ other_core, half ^ h)
+                    pl.semaphore_signal(barrier, inc=1, device_id=(grp, to), device_id_type=MESH)
+        for d in range(1, GRP):
+            pl.semaphore_signal(barrier, inc=1, device_id=(grp ^ d, seq ^ (8 * h)), device_id_type=MESH)
 
     def loads(group):
         cols = pl.ds(pl.multiple_of(group * SPAN, LANES), SPAN)
@@ -298,35 +314,32 @@
         for copy in loads(group):
             copy.wait()
         cols = pl.ds(pl.multiple_of(group * SPAN, LANES), SPAN)
-        pack_group(group, q[:, cols], k[:, cols], v[:, cols], group_mask(group), gather, send, q_pick)
+        pack_group(group, q[:, cols], k[:, cols], v[:, cols], group_mask(group), gather, send, send_pair, q_pick)
         return 0
 
     lax.fori_loop(0, GROUPS, pack, 0)
 
     pl.semaphore_wait(barrier, SEQ - 1 + 2 * (GRP - 1))
-
-    def across(j, _):
-        h = (head + j) & (HEADS - 1)
-        pltpu.make_async_remote_copy(
-            src_ref=send.at[h], dst_ref=other.at[head], send_sem=send_sem, recv_sem=recv_sem.at[1],
-            device_id=(grp, place(h, 1 - half)), device_id_type=MESH,
-        ).start()
-        return 0
-
-    def beside(j, _):
-        h = (head + j) & (HEADS - 1)
-        pltpu.make_async_remote_copy(
-            src_ref=send.at[h], dst_ref=near.at[head], send_sem=send_sem, recv_sem=recv_sem.at[0],
-            device_id=(grp, place(h, half)), device_id_type=MESH,
-        ).start()
-        return 0
 
     @pl.when(jnp.logical_not(late))
     def _():
-        lax.fori_loop(0, HEADS, across, 0)
-
-    lax.fori_loop(1, HEADS, beside, 0)
-    pltpu.make_async_copy(send.at[head], near.at[head], recv_sem.at[0]).start()
+        for offset in PLANE:
+            to = beyond(head, offset)
+            pltpu.make_async_remote_copy(
+                src_ref=send_pair.at[to >> 1], dst_ref=other.at[head >> 3, core, (head >> 1) & 3],
+                send_sem=pair_sem, recv_sem=other_sem.at[head >> 3],
+                device_id=(grp, place(to, 1 - half)), device_id_type=MESH,
+            ).start()
+
+    for offset in PLANE:
+        for other_core in (1, 0):
+            if other_core or offset != (0, 0):
+                to = beyond(head, offset) ^ other_core
+                pltpu.make_async_remote_copy(
+                    src_ref=send.at[to], dst_ref=near.at[head], send_sem=send_sem, recv_sem=near_sem,
+                    device_id=(grp, place(to, half)), device_id_type=MESH,
+                ).start()
+    pltpu.make_async_copy(send.at[head], near.at[head], near_sem).start()
 
     def local(group, _):
         cols = pl.ds(pl.multiple_of(group * SPAN, LANES), SPAN)
@@ -334,7 +347,7 @@
         local_group(group, q[:, cols], k[:, cols], v[:, cols], out)
         return 0
 
-    lax.fori_loop(0, GROUPS // 2, local, 0)
+    lax.fori_loop(0, 1, local, 0)
 
     for g in range(1, GRP):
         @pl.when(grp < g)
@@ -343,10 +356,10 @@
 
     @pl.when(half == 0)
     def _():
-        other[HEADS - 8 :] = jnp.zeros((8, PICKS, 2 * LANES), BF16)
-
-    pltpu.make_async_copy(near, near, recv_sem.at[0]).wait()
-    far_rows(head, half, grp, near, far)
+        other[3] = jnp.zeros((2, 4, PICKS, 3 * LANES), BF16)
+
+    pltpu.make_async_copy(near, near, near_sem).wait()
+    far_rows(head, half, grp, near[...].reshape(HALF_ROWS, 2 * LANES), far)
 
     def far_copy(to, h):
         return pltpu.make_async_remote_copy(
@@ -361,20 +374,27 @@
             far_copy(to, 1 - half).start()
             far_copy(to, half).start()
 
-    lax.fori_loop(GROUPS // 2, GROUPS, local, 0)
-
-    @pl.when(half == 0)
-    def _():
-        part = other.at[pl.ds(0, HEADS - 8)]
-        pltpu.make_async_copy(part, part, recv_sem.at[1]).wait()
-        far_rows(head, 1, grp, other, far)
-        coarse_blocks(head, 0, near, other, back)
-
-    @pl.when(half == 1)
-    def _():
-        pltpu.make_async_copy(other, other, recv_sem.at[1]).wait()
-        far_rows(head, 0, grp, other, far)
-        coarse_blocks(head, 1, near, other, back)
+    lax.fori_loop(1, 2, local, 0)
+
+    def pass_on(x):
+        part = other.at[x, core, :, :, pl.ds(pl.multiple_of((1 - core) * LANES, LANES), 2 * LANES)]
+        return pltpu.make_async_remote_copy(
+            src_ref=part, dst_ref=part, send_sem=pass_send.at[x], recv_sem=pass_recv.at[x],
+            device_id=(grp, seq ^ 1), device_id_type=MESH,
+        )
+
+    for part in range(2):
+        @pl.when(half == part)
+        def _():
+            for x in range(3 + part):
+                here = other.at[x, core]
+                pltpu.make_async_copy(here, here, other_sem.at[x]).wait()
+                pass_on(x).start()
+            for x in range(3 + part):
+                pass_on(x).wait()
+            y = other_keys(core, other)
+            far_rows(head, 1 - part, grp, y, far)
+            coarse_blocks(head, part, near, y, back)
 
     for g in range(GRP - 1):
         @pl.when(grp > g)
@@ -384,18 +404,20 @@
 
     whole_level(head, half, grp, far, back)
 
-    def home_copy(j, _):
-        p = (head + j) & (HEADS - 1)
-        rows = pl.ds(pl.multiple_of(p * PICKS, PICKS), PICKS)
-        pltpu.make_async_remote_copy(
-            src_ref=back.at[rows], dst_ref=home.at[head], send_sem=back_send, recv_sem=home_recv.at[head // GROUP],
-            device_id=(grp, place(p, half)), device_id_type=MESH,
-        ).start()
-        return 0
-
-    lax.fori_loop(1, HEADS, home_copy, 0)
+    for offset in PLANE:
+        for other_core in (1, 0):
+            if other_core or offset != (0, 0):
+                to = beyond(head, offset) ^ other_core
+                rows = pl.ds(pl.multiple_of(to * PICKS, PICKS), PICKS)
+                pltpu.make_async_remote_copy(
+                    src_ref=back.at[rows], dst_ref=home.at[head],
+                    send_sem=back_send, recv_sem=home_recv.at[head // GROUP],
+                    device_id=(grp, place(to, half)), device_id_type=MESH,
+                ).start()
     rows = pl.ds(pl.multiple_of(head * PICKS, PICKS), PICKS)
     pltpu.make_async_copy(back.at[rows], home.at[head], home_recv.at[head // GROUP]).start()
+
+    lax.fori_loop(2, GROUPS, local, 0)
 
     def merge(group, _):
         part = home.at[pl.ds(group * GROUP, GROUP)]
@@ -410,7 +432,7 @@
 
     @pl.when(jnp.logical_not(late))
     def _():
-        pltpu.make_async_copy(send, send, send_sem).wait()
+        pltpu.make_async_copy(send_pair, send_pair, pair_sem).wait()
 
     for to in range(1, GRP):
         @pl.when(to > grp)
@@ -435,14 +457,19 @@
             pltpu.VMEM((PICKS, WIDTH), F32),
             pltpu.VMEM((PICKS, WIDTH), F32),
             pltpu.VMEM((HEADS, PICKS, 2 * LANES), BF16),
+            pltpu.VMEM((HEADS // 2, PICKS, 3 * LANES), BF16),
             pltpu.VMEM((HEADS, PICKS, 2 * LANES), BF16),
-            pltpu.VMEM((HEADS, PICKS, 2 * LANES), BF16),
+            pltpu.VMEM((4, 2, 4, PICKS, 3 * LANES), BF16),
             pltpu.VMEM((GRP, 2, FAR, 2 * LANES), BF16),
             pltpu.VMEM((HALF_ROWS, LANES), F32),
             pltpu.VMEM((HEADS, PICKS, LANES), F32),
             pltpu.SemaphoreType.DMA((GROUPS, 3)),
             pltpu.SemaphoreType.DMA,
-            pltpu.SemaphoreType.DMA((2,)),
+            pltpu.SemaphoreType.DMA,
+            pltpu.SemaphoreType.DMA,
+            pltpu.SemaphoreType.DMA((4,)),
+            pltpu.SemaphoreType.DMA((4,)),
+            pltpu.SemaphoreType.DMA((4,)),
             pltpu.SemaphoreType.DMA((GRP, 2)),
             pltpu.SemaphoreType.DMA((GRP, 2)),
             pltpu.SemaphoreType.DMA,

time: 37.3 us -> 33.9 us (0.909)
  the two profiles are of different devices: /device:TPU:1 before, /device:TPU:64 now
where the time goes in v2:
time: 33.9 us; the launch traced here: 33.4 us
  Pallas kernels  32.3 us (95%)
  local copies, waits for them, and re-layouts  1.06 us (3%)
    pallas_call x1, Pallas kernels, body(): pl.pallas_call(kernel, out_shape=jax.ShapeDtypeStruct((ROWS, WIDTH), BF16...  32.3 us
    unnamed x1, local copies, waits for them, and re-layouts  1.06 us

profile of v2, /device:TPU:64, one launch (start us, length us, event | category | flops | bytes accessed | tf_op | source)
XLA Modules:
  0.0 33.4 jit_solution(6820384201212484990)
XLA Ops:
  0.0 32.3 %shard_map.37 = bf16[256,2560]{1,0:T(8,128)(2,1)S(1)} custom-call(bf16[256,2560]{1,0:T(8,128)(2,1)} %q_hbm.1, bf16[256,2560]{1,0:T(8,128)(2,1)} %k_hbm.1, bf16[256,2560]{1,0:T(8,128)(2,1)} %v_hbm.1), custom_call_target="tpu_custom_call" | custom-call | tf_op jit(solution)/shard_map/pallas_call | solution.py:447
  32.3 1.1 %copy.5 = bf16[256,2560]{1,0:T(8,128)(2,1)} copy(bf16[256,2560]{1,0:T(8,128)(2,1)S(1)} %shard_map.37) | data formatting | bytes 2621440

commit v3 on v2

--- a/solution.py
+++ b/solution.py
@@ -81,32 +81,42 @@
     return dot(gather, masked)
 
 
-def pack_group(group, q, k, v, mask, gather, send, send_pair, q_pick):
+def circle(x, hh):
+    tile, shift, tiles = window(hh)
+    first = x[:, LANES * tile : LANES * (tile + 1)]
+    if tiles == 1:
+        return first
+    return jnp.where(iota(first.shape, 1) >= shift, first, x[:, LANES * (tile + 1) : LANES * (tile + 2)])
+
+
+def pack_keys(group, k, v, mask, gather, send, send_pair):
     lane = iota((PICKS, LANES), 1)
-    qp, kp, vp = (pick(x, mask, gather) for x in (q, k, v))
-    q_pick[group] = qp.astype(BF16)
+    kp, vp = (pick(x, mask, gather) for x in (k, v))
     for hh in range(GROUP):
-        tile, shift, tiles = window(hh)
-
-        def circle(x):
-            first = x[:, LANES * tile : LANES * (tile + 1)]
-            if tiles == 1:
-                return first
-            return jnp.where(lane >= shift, first, x[:, LANES * (tile + 1) : LANES * (tile + 2)])
-
-        own = in_circle(lane, shift, HEAD)
-        vc = circle(vp)
+        shift = window(hh)[1]
+        vc = circle(vp, hh)
         head, pair = group * GROUP + hh, group * (GROUP // 2) + hh // 2
-        first = jnp.where(own, circle(kp), pltpu.roll(vc, HEAD, 1)).astype(BF16)
+        first = jnp.where(in_circle(lane, shift, HEAD), circle(kp, hh), pltpu.roll(vc, HEAD, 1)).astype(BF16)
         rest = pltpu.roll(vc, 32, 1)
         send[head, :, :LANES] = first
-        send[head, :, LANES:] = jnp.where(own, circle(qp), rest).astype(BF16)
+        send[head, :, LANES:] = rest.astype(BF16)
         if hh % 2 == 0:
             send_pair[pair, :, :LANES] = first
             even = jnp.where(in_circle(lane, shift + HEAD, 32), rest, 0.0)
         else:
             send_pair[pair, :, 2 * LANES :] = first
             send_pair[pair, :, LANES : 2 * LANES] = jnp.where(in_circle(lane, shift + HEAD, 32), rest, even).astype(BF16)
+
+
+def pack_queries(group, q, mask, gather, send, q_pick):
+    lane = iota((PICKS, LANES), 1)
+    qp = pick(q, mask, gather)
+    q_pick[group] = qp.astype(BF16)
+    for hh in range(GROUP):
+        head = group * GROUP + hh
+        own = in_circle(lane, window(hh)[1], HEAD)
+        rest = send[head, :, LANES:].astype(F32)
+        send[head, :, LANES:] = jnp.where(own, circle(qp, hh), rest).astype(BF16)
 
 
 def local_group(group, q, k, v, out):
@@ -211,23 +221,40 @@
 
 
 def far_rows(head, half, grp, x, far):
+    turn = lax.rem(head * HEAD, LANES)
     block = 256
     per = block // 8
     chosen = iota((per, block), 1) == iota((per, block), 0) * 8 + head // COARSE
     chosen = jnp.where(chosen, 1.0, 0.0).astype(BF16)
-    for b in range(HALF_ROWS // block):
-        far[grp, half, per * b : per * (b + 1), :] = dot(chosen, x[block * b : block * (b + 1)]).astype(BF16)
+    rows = jnp.concatenate([dot(chosen, x[block * b : block * (b + 1)]) for b in range(HALF_ROWS // block)], axis=0)
+    far[grp, half, :FAR] = rows[:, :LANES].astype(BF16)
+    rest = rows[:, LANES:]
+    packed = rest[:PICKS]
+    for i in range(1, FAR // PICKS):
+        turned = pltpu.roll(rest[PICKS * i : PICKS * (i + 1)], 32 * i, 1)
+        packed = jnp.where(in_circle(iota(packed.shape, 1), turn + HEAD + 32 * i, 32), turned, packed)
+    far[grp, half, FAR:] = packed.astype(BF16)
+    return rest.astype(BF16)
+
+
+def far_keys(far):
+    count = GRP * 2
+    first = far[:, :, :FAR].reshape(count * FAR, LANES)
+    packed = far[:, :, FAR:].astype(F32).reshape(count * PICKS, LANES)
+    turned = [packed] + [pltpu.roll(packed, LANES - 32 * i, 1) for i in range(1, FAR // PICKS)]
+    rest = jnp.stack([x.reshape(count, PICKS, LANES) for x in turned], axis=1).reshape(count * FAR, LANES)
+    return jnp.concatenate([first, rest.astype(BF16)], axis=1)
 
 
 def far_place(r):
     return (r >> 4) * 32 + (r & 15)
 
 
-def whole_level(head, half, grp, far, back):
+def whole_level(head, half, grp, far_q, far, back):
     turn = lax.rem(head * HEAD, LANES)
     own = jnp.where(in_circle(iota((1, LANES), 1), turn, HEAD), 1.0, 0.0).astype(BF16)
-    keys = far[...].reshape(GRP * 2 * FAR, 2 * LANES)
-    q = far[grp, half, :, LANES:] * own
+    keys = far_keys(far)
+    q = far_q[...] * own
 
     def hide(s):
         row, col = iota(s.shape, 0), iota(s.shape, 1)
@@ -277,7 +304,7 @@
 
 def kernel(
     q_hbm, k_hbm, v_hbm, out,
-    q, k, v, q_pick, o_pick, lse_pick, send, send_pair, near, other, far, back, home,
+    q, k, v, q_pick, o_pick, lse_pick, send, send_pair, near, other, far_q, far, back, home,
     in_sem, send_sem, pair_sem, near_sem, other_sem, pass_send, pass_recv, far_send, far_recv, back_send, home_recv,
 ):
     grp, seq = lax.axis_index("grp"), lax.axis_index("seq")
@@ -297,32 +324,52 @@
         for d in range(1, GRP):
             pl.semaphore_signal(barrier, inc=1, device_id=(grp ^ d, seq ^ (8 * h)), device_id_type=MESH)
 
-    def loads(group):
+    def load(group, n):
         cols = pl.ds(pl.multiple_of(group * SPAN, LANES), SPAN)
-        return [
-            pltpu.make_async_copy(x.at[:, cols], y.at[:, cols], in_sem.at[group, n])
-            for n, (x, y) in enumerate(((q_hbm, q), (k_hbm, k), (v_hbm, v)))
-        ]
+        x, y = ((q_hbm, q), (k_hbm, k), (v_hbm, v))[n]
+        return pltpu.make_async_copy(x.at[:, cols], y.at[:, cols], in_sem.at[group, n])
 
     for group in range(GROUPS):
-        for copy in loads(group):
-            copy.start()
+        load(group, 1).start()
+        load(group, 2).start()
+    for group in range(GROUPS):
+        load(group, 0).start()
 
     gather = jnp.where((iota((PICKS, ROWS), 1) >> 4) == iota((PICKS, ROWS), 0), 1.0, 0.0).astype(BF16)
 
     def pack(group, _):
-        for copy in loads(group):
-            copy.wait()
+        load(group, 1).wait()
+        load(group, 2).wait()
         cols = pl.ds(pl.multiple_of(group * SPAN, LANES), SPAN)
-        pack_group(group, q[:, cols], k[:, cols], v[:, cols], group_mask(group), gather, send, send_pair, q_pick)
+        pack_keys(group, k[:, cols], v[:, cols], group_mask(group), gather, send, send_pair)
         return 0
 
+    def pack_rest(group, _):
+        load(group, 0).wait()
+        cols = pl.ds(pl.multiple_of(group * SPAN, LANES), SPAN)
+        pack_queries(group, q[:, cols], group_mask(group), gather, send, q_pick)
+        return 0
+
     lax.fori_loop(0, GROUPS, pack, 0)
 
+    def local(group, _):
+        cols = pl.ds(pl.multiple_of(group * SPAN, LANES), SPAN)
+        local_picks(group, q_pick[group], k[:, cols], v[:, cols], o_pick, lse_pick)
+        local_group(group, q[:, cols], k[:, cols], v[:, cols], out)
+        return 0
+
+    ahead = jnp.where(half == 0, 2, 0)
+
+    @pl.when(half == 0)
+    def _():
+        lax.fori_loop(0, GROUPS, pack_rest, 0)
+        lax.fori_loop(0, ahead, local, 0)
+
     pl.semaphore_wait(barrier, SEQ - 1 + 2 * (GRP - 1))
 
-    @pl.when(jnp.logical_not(late))
-    def _():
+    yields = (half == 1) & (grp == GRP - 1)
+
+    def across():
         for offset in PLANE:
             to = beyond(head, offset)
             pltpu.make_async_remote_copy(
@@ -330,6 +377,14 @@
                 send_sem=pair_sem, recv_sem=other_sem.at[head >> 3],
                 device_id=(grp, place(to, 1 - half)), device_id_type=MESH,
             ).start()
+
+    @pl.when(jnp.logical_not(late | yields))
+    def _():
+        across()
+
+    @pl.when(half == 1)
+    def _():
+        lax.fori_loop(0, GROUPS, pack_rest, 0)
 
     for offset in PLANE:
         for other_core in (1, 0):
@@ -341,25 +396,23 @@
                 ).start()
     pltpu.make_async_copy(send.at[head], near.at[head], near_sem).start()
 
-    def local(group, _):
-        cols = pl.ds(pl.multiple_of(group * SPAN, LANES), SPAN)
-        local_picks(group, q_pick[group], k[:, cols], v[:, cols], o_pick, lse_pick)
-        local_group(group, q[:, cols], k[:, cols], v[:, cols], out)
-        return 0
-
-    lax.fori_loop(0, 1, local, 0)
+    @pl.when(jnp.logical_not(late) & yields)
+    def _():
+        across()
+
+    lax.fori_loop(ahead, jnp.maximum(ahead, 1), local, 0)
 
     for g in range(1, GRP):
         @pl.when(grp < g)
         def _():
-            far[g] = jnp.zeros((2, FAR, 2 * LANES), BF16)
+            far[g] = jnp.zeros((2, FAR + PICKS, LANES), BF16)
 
     @pl.when(half == 0)
     def _():
         other[3] = jnp.zeros((2, 4, PICKS, 3 * LANES), BF16)
 
     pltpu.make_async_copy(near, near, near_sem).wait()
-    far_rows(head, half, grp, near[...].reshape(HALF_ROWS, 2 * LANES), far)
+    far_q[...] = far_rows(head, half, grp, near[...].reshape(HALF_ROWS, 2 * LANES), far)
 
     def far_copy(to, h):
         return pltpu.make_async_remote_copy(
@@ -374,7 +427,7 @@
             far_copy(to, 1 - half).start()
             far_copy(to, half).start()
 
-    lax.fori_loop(1, 2, local, 0)
+    lax.fori_loop(jnp.maximum(ahead, 1), jnp.maximum(ahead, 2), local, 0)
 
     def pass_on(x):
         part = other.at[x, core, :, :, pl.ds(pl.multiple_of((1 - core) * LANES, LANES), 2 * LANES)]
@@ -402,7 +455,7 @@
             for h in range(2):
                 pltpu.make_async_copy(far.at[g, h], far.at[g, h], far_recv.at[g, h]).wait()
 
-    whole_level(head, half, grp, far, back)
+    whole_level(head, half, grp, far_q, far, back)
 
     for offset in PLANE:
         for other_core in (1, 0):
@@ -417,7 +470,7 @@
     rows = pl.ds(pl.multiple_of(head * PICKS, PICKS), PICKS)
     pltpu.make_async_copy(back.at[rows], home.at[head], home_recv.at[head // GROUP]).start()
 
-    lax.fori_loop(2, GROUPS, local, 0)
+    lax.fori_loop(jnp.maximum(ahead, 2), GROUPS, local, 0)
 
     def merge(group, _):
         part = home.at[pl.ds(group * GROUP, GROUP)]
@@ -460,7 +513,8 @@
             pltpu.VMEM((HEADS // 2, PICKS, 3 * LANES), BF16),
             pltpu.VMEM((HEADS, PICKS, 2 * LANES), BF16),
             pltpu.VMEM((4, 2, 4, PICKS, 3 * LANES), BF16),
-            pltpu.VMEM((GRP, 2, FAR, 2 * LANES), BF16),
+            pltpu.VMEM((FAR, LANES), BF16),
+            pltpu.VMEM((GRP, 2, FAR + PICKS, LANES), BF16),
             pltpu.VMEM((HALF_ROWS, LANES), F32),
             pltpu.VMEM((HEADS, PICKS, LANES), F32),
             pltpu.SemaphoreType.DMA((GROUPS, 3)),

time: 33.9 us -> 32.9 us (0.971); the launches traced: 33.4 us -> 32.9 us
  Pallas kernels: 32.3 us -> 31.8 us
    pallas_call x1, Pallas kernels: 32.3 us -> 31.8 us  [body(): pl.pallas_call(kernel, out_shape=jax.ShapeDtypeStruct((ROWS, WIDTH), BF16...]
where the time goes in v3:
time: 32.9 us
  Pallas kernels  31.8 us (97%)
  local copies, waits for them, and re-layouts  1.06 us (3%)
    pallas_call x1, Pallas kernels, body(): pl.pallas_call(kernel, out_shape=jax.ShapeDtypeStruct((ROWS, WIDTH), BF16...  31.8 us
    unnamed x1, local copies, waits for them, and re-layouts  1.06 us

profile of v3, /device:TPU:64, one launch (start us, length us, event | category | flops | bytes accessed | tf_op | source)
XLA Modules:
  0.0 32.9 jit_solution(13742903353867265255)
XLA Ops:
  0.0 31.8 %shard_map.37 = bf16[256,2560]{1,0:T(8,128)(2,1)S(1)} custom-call(bf16[256,2560]{1,0:T(8,128)(2,1)} %q_hbm.1, bf16[256,2560]{1,0:T(8,128)(2,1)} %k_hbm.1, bf16[256,2560]{1,0:T(8,128)(2,1)} %v_hbm.1), custom_call_target="tpu_custom_call" | custom-call | tf_op jit(solution)/shard_map/pallas_call | solution.py:500
  31.8 1.1 %copy.5 = bf16[256,2560]{1,0:T(8,128)(2,1)} copy(bf16[256,2560]{1,0:T(8,128)(2,1)S(1)} %shard_map.37) | data formatting | bytes 2621440

commit v4 on v3

--- a/solution.py
+++ b/solution.py
@@ -179,8 +179,14 @@
 
 
 def attend(q, parts, lane, turn):
-    scores = [hide(dot(q, keys[:, :LANES], NT)) for keys, hide in parts]
-    top = functools.reduce(jnp.maximum, [jnp.max(s, axis=1, keepdims=True) for s in scores])
+    scores, tops = [], []
+    for keys, known in parts:
+        if callable(known):
+            s = known(dot(q, keys[:, :LANES], NT))
+            known = s, jnp.max(s, axis=1, keepdims=True)
+        scores.append(known[0])
+        tops.append(known[1])
+    top = functools.reduce(jnp.maximum, tops)
     weights = [jnp.exp2((s - top) * (SCALE * LOG2E)) for s in scores]
     mass = sum(jnp.sum(w, axis=1, keepdims=True) for w in weights)
     both = sum(dot(w.astype(BF16), keys) for w, (keys, _) in zip(weights, parts))
@@ -200,24 +206,34 @@
     return jnp.concatenate([x.reshape(HALF_ROWS, LANES) for x in (first, rest)], axis=1)
 
 
-def coarse_blocks(head, half, near, y, back):
+STEP = 128
+
+
+def near_scores(head, near, scores, tops):
     turn = lax.rem(head * HEAD, LANES)
     own = jnp.where(in_circle(iota((1, LANES), 1), turn, HEAD), 1.0, 0.0).astype(BF16)
-    step = 128
-    below = iota((step, step), 1) <= iota((step, step), 0)
+    below = iota((STEP, STEP), 1) <= iota((STEP, STEP), 0)
     x = near[...].reshape(HALF_ROWS, 2 * LANES)
-    for b in range(HALF_ROWS // step):
-        start = b * step
-
-        def last_hidden(s):
-            last = jnp.where(below, s[:, start:], LOWEST)
-            return last if b == 0 else jnp.concatenate([s[:, :start], last], axis=1)
-
-        parts = [(x[: start + step], last_hidden)]
+    for start in range(0, HALF_ROWS, STEP):
+        end = start + STEP
+        s = dot(x[start:end, LANES:] * own, x[:end, :LANES], NT)
+        last = jnp.where(below, s[:, start:], LOWEST)
+        s = last if start == 0 else jnp.concatenate([s[:, :start], last], axis=1)
+        scores[start:end, :end] = s
+        tops[start:end, :] = jnp.broadcast_to(jnp.max(s, axis=1, keepdims=True), (STEP, LANES))
+
+
+def coarse_blocks(head, half, near, y, scores, tops, back):
+    turn = lax.rem(head * HEAD, LANES)
+    own = jnp.where(in_circle(iota((1, LANES), 1), turn, HEAD), 1.0, 0.0).astype(BF16)
+    x = near[...].reshape(HALF_ROWS, 2 * LANES)
+    for b in range(HALF_ROWS // STEP):
+        start, end = b * STEP, (b + 1) * STEP
+        parts = [(x[:end], (scores[start:end, :end], tops[start:end, :1]))]
         if b + half > 0:
-            parts.append((y[: start + half * step], lambda s: s))
-        q = x[start : start + step, LANES:] * own
-        back[start : start + step, :] = attend(q, parts, iota((step, LANES), 1), turn)
+            parts.append((y[: start + half * STEP], lambda s: s))
+        q = x[start:end, LANES:] * own
+        back[start:end, :] = attend(q, parts, iota((STEP, LANES), 1), turn)
 
 
 def far_rows(head, half, grp, x, far):
@@ -304,7 +320,7 @@
 
 def kernel(
     q_hbm, k_hbm, v_hbm, out,
-    q, k, v, q_pick, o_pick, lse_pick, send, send_pair, near, other, far_q, far, back, home,
+    q, k, v, q_pick, o_pick, lse_pick, send, send_pair, near, other, far_q, far, scores, tops, back, home,
     in_sem, send_sem, pair_sem, near_sem, other_sem, pass_send, pass_recv, far_send, far_recv, back_send, home_recv,
 ):
     grp, seq = lax.axis_index("grp"), lax.axis_index("seq")
@@ -427,6 +443,7 @@
             far_copy(to, 1 - half).start()
             far_copy(to, half).start()
 
+    near_scores(head, near, scores, tops)
     lax.fori_loop(jnp.maximum(ahead, 1), jnp.maximum(ahead, 2), local, 0)
 
     def pass_on(x):
@@ -447,7 +464,7 @@
                 pass_on(x).wait()
             y = other_keys(core, other)
             far_rows(head, 1 - part, grp, y, far)
-            coarse_blocks(head, part, near, y, back)
+            coarse_blocks(head, part, near, y, scores, tops, back)
 
     for g in range(GRP - 1):
         @pl.when(grp > g)
@@ -515,6 +532,8 @@
             pltpu.VMEM((4, 2, 4, PICKS, 3 * LANES), BF16),
             pltpu.VMEM((FAR, LANES), BF16),
             pltpu.VMEM((GRP, 2, FAR + PICKS, LANES), BF16),
+            pltpu.VMEM((HALF_ROWS, HALF_ROWS), F32),
+            pltpu.VMEM((HALF_ROWS, LANES), F32),
             pltpu.VMEM((HALF_ROWS, LANES), F32),
             pltpu.VMEM((HEADS, PICKS, LANES), F32),
             pltpu.SemaphoreType.DMA((GROUPS, 3)),

time: 32.9 us -> 32.6 us (level)
    pallas_call x1, Pallas kernels: 31.8 us -> 31.5 us  [body(): pl.pallas_call(kernel, out_shape=jax.ShapeDtypeStruct((ROWS, WIDTH), BF16...]
where the time goes in v4:
time: 32.6 us; the launch traced here: 32.5 us
  Pallas kernels  31.5 us (97%)
  local copies, waits for them, and re-layouts  1.06 us (3%)
    pallas_call x1, Pallas kernels, body(): pl.pallas_call(kernel, out_shape=jax.ShapeDtypeStruct((ROWS, WIDTH), BF16...  31.5 us
    unnamed x1, local copies, waits for them, and re-layouts  1.06 us

profile of v4, /device:TPU:64, one launch (start us, length us, event | category | flops | bytes accessed | tf_op | source)
XLA Modules:
  0.0 32.5 jit_solution(14951653125934536244)
XLA Ops:
  0.0 31.5 %shard_map.37 = bf16[256,2560]{1,0:T(8,128)(2,1)S(1)} custom-call(bf16[256,2560]{1,0:T(8,128)(2,1)} %q_hbm.1, bf16[256,2560]{1,0:T(8,128)(2,1)} %k_hbm.1, bf16[256,2560]{1,0:T(8,128)(2,1)} %v_hbm.1), custom_call_target="tpu_custom_call" | custom-call | tf_op jit(solution)/shard_map/pallas_call | solution.py:517
  31.5 1.1 %copy.5 = bf16[256,2560]{1,0:T(8,128)(2,1)} copy(bf16[256,2560]{1,0:T(8,128)(2,1)S(1)} %shard_map.37) | data formatting | bytes 2621440

commit v5 on v4

--- a/solution.py
+++ b/solution.py
@@ -385,8 +385,8 @@
 
     yields = (half == 1) & (grp == GRP - 1)
 
-    def across():
-        for offset in PLANE:
+    def across(offsets):
+        for offset in offsets:
             to = beyond(head, offset)
             pltpu.make_async_remote_copy(
                 src_ref=send_pair.at[to >> 1], dst_ref=other.at[head >> 3, core, (head >> 1) & 3],
@@ -394,9 +394,15 @@
                 device_id=(grp, place(to, 1 - half)), device_id_type=MESH,
             ).start()
 
+    splits = (half == 1) & (grp == 0)
+
     @pl.when(jnp.logical_not(late | yields))
     def _():
-        across()
+        across(PLANE[:8])
+
+    @pl.when(jnp.logical_not(late | yields | splits))
+    def _():
+        across(PLANE[8:])
 
     @pl.when(half == 1)
     def _():
@@ -414,7 +420,11 @@
 
     @pl.when(jnp.logical_not(late) & yields)
     def _():
-        across()
+        across(PLANE[:8])
+
+    @pl.when(jnp.logical_not(late) & (yields | splits))
+    def _():
+        across(PLANE[8:])
 
     lax.fori_loop(ahead, jnp.maximum(ahead, 1), local, 0)
 
@@ -440,8 +450,8 @@
     for to in range(1, GRP):
         @pl.when(to > grp)
         def _():
+            far_copy(to, half).start()
             far_copy(to, 1 - half).start()
-            far_copy(to, half).start()
 
     near_scores(head, near, scores, tops)
     lax.fori_loop(jnp.maximum(ahead, 1), jnp.maximum(ahead, 2), local, 0)

time: 32.6 us -> 32.6 us (level)
  no operation moved by 1% of the time
where the time goes in v5:
time: 32.6 us; the launch traced here: 32.5 us
  Pallas kernels  31.5 us (97%)
  local copies, waits for them, and re-layouts  1.06 us (3%)
    pallas_call x1, Pallas kernels, body(): pl.pallas_call(kernel, out_shape=jax.ShapeDtypeStruct((ROWS, WIDTH), BF16...  31.5 us
    unnamed x1, local copies, waits for them, and re-layouts  1.06 us

profile of v5, /device:TPU:64, one launch (start us, length us, event | category | flops | bytes accessed | tf_op | source)
XLA Modules:
  0.0 32.5 jit_solution(7411722095797280049)
XLA Ops:
  0.0 31.5 %shard_map.37 = bf16[256,2560]{1,0:T(8,128)(2,1)S(1)} custom-call(bf16[256,2560]{1,0:T(8,128)(2,1)} %q_hbm.1, bf16[256,2560]{1,0:T(8,128)(2,1)} %k_hbm.1, bf16[256,2560]{1,0:T(8,128)(2,1)} %v_hbm.1), custom_call_target="tpu_custom_call" | custom-call | tf_op jit(solution)/shard_map/pallas_call | solution.py:527
  31.5 1.1 %copy.5 = bf16[256,2560]{1,0:T(8,128)(2,1)} copy(bf16[256,2560]{1,0:T(8,128)(2,1)S(1)} %shard_map.37) | data formatting | bytes 2621440
